TPU v7x, 128 devices: a whole 4x4x4 slice. The times are simulated.
128 devices in a mesh: row: 8 (over y, x_hi), col: 16 (over z, x_lo, core).
Axes of the slice: x: 4 (x_hi: 2, x_lo: 2; x = x_hi * 2 + x_lo), y: 4, z: 4, core: 2. Of those that a mesh axis runs over, the one named last changes fastest.
Arguments:
- new_row: float32 [128, 192, 128], P('row', 'col'), may hold values from -4 to 4
- history: float32 [192, 192, 128, 128], P('row', 'col'), may hold values from -0.0390625 to 0.0390625
- hamiltonian: float32 [128, 128], replicated, may hold values from -0.5 to 0.5
Outputs:
- rows_out: float32 [3, 128, 192, 128], P(None, 'row', 'col')
All inputs are finite; a program needn't handle non-finite values.
Results may differ from a plain program's by a relative error of at most 0.00026.
Values sent between devices are 32-bit elements; how exact they have to be, the bound alone decides.
A program may use at most 128 MiB of HBM per device.

v0:
```python
import jax
import jax.numpy as jnp
from jax import lax
from jax.sharding import PartitionSpec as P

STEPS = 3
time_step = 0.2


def sigma_panel(sigma_all, tile_rows):
    row_start = lax.axis_index("row") * tile_rows
    gathered = lax.all_gather(sigma_all, "col", axis=1, tiled=True)
    return lax.dynamic_slice_in_dim(gathered, row_start, tile_rows, 1)


def contract(sigma_rows, history):
    return jnp.einsum(
        "isl,stlj->itj",
        sigma_rows,
        history,
        precision=lax.Precision.HIGHEST,
        preferred_element_type=jnp.float32,
    )


def advance(current, hamiltonian, collision):
    kinetic = jnp.einsum(
        "itl,lj->itj",
        current,
        hamiltonian,
        precision=lax.Precision.HIGHEST,
        preferred_element_type=jnp.float32,
    )
    return current - time_step * (kinetic + collision)


def per_device(new_row, history, hamiltonian):
    tile_rows = history.shape[0]
    results = []
    current = new_row
    for step_index in range(STEPS):
        sigma_local = current * current * current
        sigma_all = lax.all_gather(sigma_local, "row", axis=0, tiled=True)
        sigma_rows = sigma_panel(sigma_all, tile_rows)
        collision = lax.psum_scatter(
            contract(sigma_rows, history), "row", scatter_dimension=0, tiled=True
        )
        current = advance(current, hamiltonian, collision)
        results.append(current)
    return jnp.stack(results)


def solution(mesh):
    placed = (P("row", "col", None), P("row", "col", None, None), P())
    return jax.shard_map(
        per_device,
        mesh=mesh,
        in_specs=placed,
        out_specs=P(None, "row", "col", None),
        check_vma=False,
    )
```

profile of v0, /device:TPU:0, one launch (start us, length us, event | category | flops | bytes accessed | tf_op | source)
XLA Modules:
  0.0 612.5 jit_solution(13961219519606241692)
XLA Ops:
  6.5 0.0 copy-start
  6.5 0.0 copy-start.1
  6.5 0.0 all-gather.4.cloned.1.call-start
  6.5 1.0 multiply_multiply_fusion.2
  7.5 38.7 %all_gather.18 = f32[128,12,128]{2,0,1:T(8,128)} all-gather(f32[16,12,128]{2,0,1:T(8,128)S(1)} %multiply_multiply_fusion.2), channel_id=1, replica_groups=mesh['row'=8,'col'=16] {'row'}, dimensions={0}, use_global_device_ids=true | all-gather | bytes 884736 | tf_op jit(solution)/shard_map/all_gather | solution.py:43
  46.2 0.0 all-gather.4.cloned.1.call-update
  46.2 0.0 reduce-scatter.4.cloned.1.call-start
  46.3 74.7 %all-gather.4.cloned.1.call-done = f32[128,192,128]{2,0,1:T(8,128)} async-done(((f32[128,12,128]{2,0,1:T(8,128)}), f32[128,192,128]{2,0,1:T(8,128)}) %all-gather.4.cloned.1.call-update) | async-done | bytes 12582928 | tf_op jit(solution)/shard_map/all_gather | solution.py:12
  121.0 14.3 %fusion.9 = f32[128,12,128]{2,0,1:T(8,128)} fusion(f32[24,12,128,128]{3,2,1,0:T(8,128)} %param.4, f32[128,192,128]{2,0,1:T(8,128)} %all-gather.4.cloned.1.call-done, s32[]{:T(128)S(6)} %select_n.2), kind=kOutput, calls=%fused_computation.9 | convolution fusion | flops 7247757312 | bytes 21233668 | tf_op jit(solution)/shard_map/isl,stlj->itj/dot_general | solution.py:17
  135.3 0.0 reduce-scatter.4.cloned.1.call-update
  135.3 0.0 all-gather.6.cloned.1.call-start
  135.4 72.5 %reduce-scatter.4.cloned.1.call-done = f32[16,12,128]{2,0,1:T(8,128)} async-done(((f32[128,12,128]{2,0,1:T(8,128)}), f32[16,12,128]{2,0,1:T(8,128)}) %reduce-scatter.4.cloned.1.call-update) | async-done | bytes 98320 | tf_op jit(solution)/shard_map/reduce_scatter | solution.py:45
  207.8 0.0 copy-done
  207.9 0.0 copy-done.1
  207.9 1.1 multiply_multiply_fusion.1
  209.0 38.9 %all_gather.20 = f32[128,12,128]{2,0,1:T(8,128)} all-gather(f32[16,12,128]{2,0,1:T(8,128)S(1)} %get-tuple-element.5), channel_id=1, replica_groups=mesh['row'=8,'col'=16] {'row'}, dimensions={0}, use_global_device_ids=true | all-gather | bytes 884736 | tf_op jit(solution)/shard_map/all_gather | solution.py:43
  247.9 0.0 all-gather.6.cloned.1.call-update
  247.9 0.0 reduce-scatter.6.cloned.1.call-start
  248.0 71.0 %all-gather.6.cloned.1.call-done = f32[128,192,128]{2,0,1:T(8,128)} async-done(((f32[128,12,128]{2,0,1:T(8,128)}), f32[128,192,128]{2,0,1:T(8,128)}) %all-gather.6.cloned.1.call-update) | async-done | bytes 12582928 | tf_op jit(solution)/shard_map/all_gather | solution.py:12
  319.0 14.3 %fusion.12 = f32[128,12,128]{2,0,1:T(8,128)} fusion(f32[24,12,128,128]{3,2,1,0:T(8,128)} %param.4, f32[128,192,128]{2,0,1:T(8,128)} %all-gather.6.cloned.1.call-done, s32[]{:T(128)S(6)} %select_n.2), kind=kOutput, calls=%fused_computation.10 | convolution fusion | flops 7247757312 | bytes 21233668 | tf_op jit(solution)/shard_map/isl,stlj->itj/dot_general | solution.py:17
  333.3 0.0 reduce-scatter.6.cloned.1.call-update
  333.3 0.0 all-gather.8.cloned.1.call-start
  333.4 72.5 %reduce-scatter.6.cloned.1.call-done = f32[16,12,128]{2,0,1:T(8,128)} async-done(((f32[128,12,128]{2,0,1:T(8,128)}), f32[16,12,128]{2,0,1:T(8,128)}) %reduce-scatter.6.cloned.1.call-update) | async-done | bytes 98320 | tf_op jit(solution)/shard_map/reduce_scatter | solution.py:45
  405.9 1.1 multiply_multiply_fusion
  407.0 38.9 %all_gather.22 = f32[128,12,128]{2,0,1:T(8,128)} all-gather(f32[16,12,128]{2,0,1:T(8,128)S(1)} %get-tuple-element.7), channel_id=1, replica_groups=mesh['row'=8,'col'=16] {'row'}, dimensions={0}, use_global_device_ids=true | all-gather | bytes 884736 | tf_op jit(solution)/shard_map/all_gather | solution.py:43
  445.9 0.0 all-gather.8.cloned.1.call-update
  445.9 0.2 reduce-scatter.8.cloned.1.call-start
  446.2 70.8 %all-gather.8.cloned.1.call-done = f32[128,192,128]{2,0,1:T(8,128)} async-done(((f32[128,12,128]{2,0,1:T(8,128)}), f32[128,192,128]{2,0,1:T(8,128)}) %all-gather.8.cloned.1.call-update) | async-done | bytes 12582928 | tf_op jit(solution)/shard_map/all_gather | solution.py:12
  516.9 14.3 %fusion.15 = f32[128,12,128]{2,0,1:T(8,128)} fusion(f32[24,12,128,128]{3,2,1,0:T(8,128)} %param.4, f32[128,192,128]{2,0,1:T(8,128)} %all-gather.8.cloned.1.call-done, s32[]{:T(128)S(6)} %select_n.2), kind=kOutput, calls=%fused_computation.11 | convolution fusion | flops 7247757312 | bytes 21233668 | tf_op jit(solution)/shard_map/isl,stlj->itj/dot_general | solution.py:17
  531.3 0.0 reduce-scatter.8.cloned.1.call-update
  531.3 72.5 %reduce-scatter.8.cloned.1.call-done = f32[16,12,128]{2,0,1:T(8,128)} async-done(((f32[128,12,128]{2,0,1:T(8,128)}), f32[16,12,128]{2,0,1:T(8,128)}) %reduce-scatter.8.cloned.1.call-update) | async-done | bytes 98320 | tf_op jit(solution)/shard_map/reduce_scatter | solution.py:45
  603.8 1.1 fusion.20
  604.9 0.7 pad_maximum_fusion
Async XLA Ops:
  6.5 201.3 %copy-start = (f32[128,128]{1,0:T(8,128)S(1)}, f32[128,128]{1,0:T(8,128)}, u32[]{:S(2)}) copy-start(f32[128,128]{1,0:T(8,128)} %param.5) | copy-start | bytes 196612
  6.5 201.3 %copy-start.1 = (f32[16,12,128]{2,0,1:T(8,128)S(1)}, f32[16,12,128]{2,0,1:T(8,128)}, u32[]{:S(2)}) copy-start(f32[16,12,128]{2,0,1:T(8,128)} %param.3) | copy-start | bytes 294916
  6.5 114.4 %all-gather.4.cloned.1.call-start = ((), (), s32[]{:S(2)}) async-start(), calls=%async_computation.3 | async-start | bytes 13369344 | tf_op jit(solution)/shard_map/all_gather | solution.py:12
  46.2 161.7 %reduce-scatter.4.cloned.1.call-start = ((), (), s32[]{:S(2)}) async-start(), calls=%async_computation.4 | async-start | bytes 884736 | tf_op jit(solution)/shard_map/reduce_scatter | solution.py:45
  135.3 183.6 %all-gather.6.cloned.1.call-start = ((), (), s32[]{:S(2)}) async-start(), calls=%async_computation.5 | async-start | bytes 13369344 | tf_op jit(solution)/shard_map/all_gather | solution.py:12
  247.9 157.9 %reduce-scatter.6.cloned.1.call-start = ((), (), s32[]{:S(2)}) async-start(), calls=%async_computation.6 | async-start | bytes 884736 | tf_op jit(solution)/shard_map/reduce_scatter | solution.py:45
  333.3 183.6 %all-gather.8.cloned.1.call-start = ((), (), s32[]{:S(2)}) async-start(), calls=%async_computation.7 | async-start | bytes 13369344 | tf_op jit(solution)/shard_map/all_gather | solution.py:12
  445.9 157.9 %reduce-scatter.8.cloned.1.call-start = ((), (), s32[]{:S(2)}) async-start(), calls=%async_computation.8 | async-start | bytes 884736 | tf_op jit(solution)/shard_map/reduce_scatter | solution.py:45
Sparse Core Ops, SparseCore 0:
  46.3 74.6 all-gather.3
  135.4 72.3 reduce-scatter.3
  248.1 70.8 all-gather.5
  333.4 72.3 reduce-scatter.5
  446.1 70.8 all-gather.7
  531.4 72.3 reduce-scatter.7
where the time goes:
time: 613 us
  waiting for transfers between devices  434 us (71%)
  blocking collectives  116 us (19%)
  matrix products  46.4 us (8%)
  between operations  13.5 us (2%)
    reduce_scatter x3, waiting for transfers between devices, per_device(): lax.psum_scatter(contract(sigma_rows, history), 'row', scatter_dimension=...  217 us
    all_gather x3, waiting for transfers between devices, sigma_panel(): gathered = lax.all_gather(sigma_all, 'col', axis=1, tiled=True)  216 us
    all_gather x3, blocking collectives, per_device(): sigma_all = lax.all_gather(sigma_local, 'row', axis=0, tiled=True)  116 us
    dot_general x3, matrix products, contract(): jnp.einsum('isl,stlj->itj', sigma_rows, history, precision=lax.Precision....  43 us
  transfers between devices with their start and end apart: 6, of which 6 were waited for; matrix products, arithmetic and copies ran while one was open for 0% of the time, Pallas kernels for 0%

commit v1 on v0

--- a/solution.py
+++ b/solution.py
@@ -9,7 +9,9 @@
 
 def sigma_panel(sigma_all, tile_rows):
     row_start = lax.axis_index("row") * tile_rows
-    gathered = lax.all_gather(sigma_all, "col", axis=1, tiled=True)
+    gathered = jnp.concatenate(
+        lax.all_to_all(jnp.stack([sigma_all] * lax.axis_size("col")), "col", 0, 0), axis=1
+    )
     return lax.dynamic_slice_in_dim(gathered, row_start, tile_rows, 1)
 
 

time: 613 us -> 825 us (1.35)
  blocking collectives: 116 us -> 401 us
  waiting for transfers between devices: 434 us -> 349 us
  local copies, waits for them, and re-layouts: 0.01 us -> 9.33 us
    all_to_all x0 -> x2, blocking collectives: none -> 290 us  [sigma_panel(): lax.all_to_all(jnp.stack([sigma_all] * lax.axis_size('col')), 'col', 0, 0)]
    all_gather x3 -> x0, waiting for transfers between devices: 216 us -> none  [sigma_panel(): gathered = lax.all_gather(sigma_all, 'col', axis=1, tiled=True)]
    all_to_all x0 -> x1, waiting for transfers between devices: none -> 140 us  [sigma_panel(): lax.all_to_all(jnp.stack([sigma_all] * lax.axis_size('col')), 'col', 0, 0)]
    another operation x0 -> x3, local copies, waits for them, and re-layouts: none -> 9.27 us  [sigma_panel(): jnp.stack([sigma_all] * lax.axis_size('col'))]
    reduce_scatter x3, waiting for transfers between devices: 217 us -> 209 us  [per_device(): lax.psum_scatter(contract(sigma_rows, history), 'row', scatter_dimension=...]
  transfers between devices with their start and end apart: 6 -> 4, of which waited for: 6 -> 4; matrix products, arithmetic and copies ran while one was open for 0% -> 0% of each run, Pallas kernels for 0% -> 0%
where the time goes in v1:
time: 825 us; the launch traced here: 824 us
  blocking collectives  401 us (49%)
  waiting for transfers between devices  349 us (42%)
  matrix products  42.7 us (5%)
  between operations  13.3 us (2%)
  local copies, waits for them, and re-layouts  9.33 us (1%)
    all_to_all x2, blocking collectives, sigma_panel(): lax.all_to_all(jnp.stack([sigma_all] * lax.axis_size('col')), 'col', 0, 0)  290 us
    reduce_scatter x3, waiting for transfers between devices, per_device(): lax.psum_scatter(contract(sigma_rows, history), 'row', scatter_dimension=...  209 us
    all_to_all x1, waiting for transfers between devices, sigma_panel(): lax.all_to_all(jnp.stack([sigma_all] * lax.axis_size('col')), 'col', 0, 0)  140 us
    all_gather x3, blocking collectives, per_device(): sigma_all = lax.all_gather(sigma_local, 'row', axis=0, tiled=True)  111 us
    dot_general x3, matrix products, contract(): jnp.einsum('isl,stlj->itj', sigma_rows, history, precision=lax.Precision....  39.3 us
  transfers between devices with their start and end apart: 4, of which 4 were waited for; matrix products, arithmetic and copies ran while one was open for 0% of the time, Pallas kernels for 0%

profile of v1, /device:TPU:0, one launch (start us, length us, event | category | flops | bytes accessed | tf_op | source)
XLA Modules:
  0.0 824.1 jit_solution(10472859751470623291)
XLA Ops:
  6.5 0.0 copy-start
  6.5 0.9 multiply_multiply_fusion.2
  7.5 37.0 %all_gather.9 = f32[128,12,128]{2,0,1:T(8,128)S(1)} all-gather(f32[16,12,128]{2,0,1:T(8,128)S(1)} %multiply_multiply_fusion.2), channel_id=1, replica_groups=mesh['row'=8,'col'=16] {'row'}, dimensions={0}, use_global_device_ids=true | all-gather | bytes 884736 | tf_op jit(solution)/shard_map/all_gather | solution.py:45
  44.5 6.1 stack.14
  50.6 6.9 all-to-all-start
  57.5 0.0 copy-start.1
  57.5 0.0 reduce-scatter.4.cloned.1.call-start
  57.6 140.2 %all-to-all-done = f32[16,128,12,128]{3,1,2,0:T(8,128)} async-done(((f32[16,128,12,128]{3,1,2,0:T(8,128)}), f32[16,128,12,128]{3,1,2,0:T(8,128)}, u32[]{:S(2)}, u32[]{:S(2)}) %all-to-all-start) | async-done | bytes 12582944 | tf_op jit(solution)/shard_map/all_to_all | solution.py:13
  197.8 14.3 %fusion.9 = f32[128,12,128]{2,0,1:T(8,128)} fusion(f32[24,12,128,128]{3,2,1,0:T(8,128)} %param.4, f32[128,192,128]{2,0,1:T(8,128)} %bitcast.2, s32[]{:T(128)S(6)} %select_n.2), kind=kOutput, calls=%fused_computation.9 | convolution fusion | flops 7247757312 | bytes 21233668 | tf_op jit(solution)/shard_map/isl,stlj->itj/dot_general | solution.py:19
  212.1 0.0 reduce-scatter.4.cloned.1.call-update
  212.1 0.0 reduce-scatter.6.cloned.1.call-start
  212.2 70.5 %reduce-scatter.4.cloned.1.call-done = f32[16,12,128]{2,0,1:T(8,128)} async-done(((f32[128,12,128]{2,0,1:T(8,128)}), f32[16,12,128]{2,0,1:T(8,128)}) %reduce-scatter.4.cloned.1.call-update) | async-done | bytes 98320 | tf_op jit(solution)/shard_map/reduce_scatter | solution.py:47
  282.7 0.0 copy-done
  282.7 0.0 copy-done.1
  282.7 1.1 multiply_multiply_fusion.1
  283.9 37.2 %all_gather.10 = f32[128,12,128]{2,0,1:T(8,128)S(1)} all-gather(f32[16,12,128]{2,0,1:T(8,128)S(1)} %get-tuple-element.5), channel_id=1, replica_groups=mesh['row'=8,'col'=16] {'row'}, dimensions={0}, use_global_device_ids=true | all-gather | bytes 884736 | tf_op jit(solution)/shard_map/all_gather | solution.py:45
  321.1 0.0 slice-start
  321.1 1.6 stack.16
  322.7 0.0 slice-start.2
  322.7 0.0 slice-start.3
  322.7 0.0 slice-start.4
  322.7 144.8 %all_to_all.15 = f32[16,128,12,128]{3,1,2,0:T(8,128)} all-to-all(f32[16,128,12,128]{3,1,2,0:T(8,128)S(1)} %stack.16), channel_id=1, replica_groups=mesh['row'=8,'col'=16] {'col'}, dimensions={0} | all-to-all | bytes 25165824 | tf_op jit(solution)/shard_map/all_to_all | solution.py:13
  467.5 0.0 slice-done
  467.5 0.0 slice-done.1
  467.5 0.0 slice-done.2
  467.5 0.0 slice-done.3
  467.5 0.0 slice-done.4
  467.6 12.5 %fusion.12 = f32[128,12,128]{2,0,1:T(8,128)} fusion(f32[24,12,128,128]{3,2,1,0:T(8,128)S(1)} %bitcast.67, f32[128,192,128]{2,0,1:T(8,128)} %bitcast.71, s32[]{:T(128)S(6)} %select_n.2), kind=kOutput, calls=%fused_computation.10 | convolution fusion | flops 7247757312 | bytes 21233668 | tf_op jit(solution)/shard_map/isl,stlj->itj/dot_general | solution.py:19
  480.1 0.0 reduce-scatter.6.cloned.1.call-update
  480.1 0.0 reduce-scatter.8.cloned.1.call-start
  480.1 69.1 %reduce-scatter.6.cloned.1.call-done = f32[16,12,128]{2,0,1:T(8,128)} async-done(((f32[128,12,128]{2,0,1:T(8,128)}), f32[16,12,128]{2,0,1:T(8,128)}) %reduce-scatter.6.cloned.1.call-update) | async-done | bytes 98320 | tf_op jit(solution)/shard_map/reduce_scatter | solution.py:47
  549.2 1.1 multiply_multiply_fusion
  550.4 37.3 %all_gather.11 = f32[128,12,128]{2,0,1:T(8,128)S(1)} all-gather(f32[16,12,128]{2,0,1:T(8,128)S(1)} %get-tuple-element.7), channel_id=1, replica_groups=mesh['row'=8,'col'=16] {'row'}, dimensions={0}, use_global_device_ids=true | all-gather | bytes 884736 | tf_op jit(solution)/shard_map/all_gather | solution.py:45
  587.6 1.6 stack.18
  589.2 0.0 slice-start.7
  589.2 0.0 slice-start.8
  589.2 0.0 slice-start.9
  589.2 144.8 %all_to_all.16 = f32[16,128,12,128]{3,1,2,0:T(8,128)} all-to-all(f32[16,128,12,128]{3,1,2,0:T(8,128)S(1)} %stack.18), channel_id=1, replica_groups=mesh['row'=8,'col'=16] {'col'}, dimensions={0} | all-to-all | bytes 25165824 | tf_op jit(solution)/shard_map/all_to_all | solution.py:13
  734.0 0.0 slice-done.5
  734.0 0.0 slice-done.6
  734.0 0.0 slice-done.7
  734.0 0.0 slice-done.8
  734.0 0.0 slice-done.9
  734.0 12.5 %fusion.15 = f32[128,12,128]{2,0,1:T(8,128)} fusion(f32[24,12,128,128]{3,2,1,0:T(8,128)S(1)} %bitcast.69, f32[128,192,128]{2,0,1:T(8,128)} %bitcast.70, s32[]{:T(128)S(6)} %select_n.2), kind=kOutput, calls=%fused_computation.11 | convolution fusion | flops 7247757312 | bytes 21233668 | tf_op jit(solution)/shard_map/isl,stlj->itj/dot_general | solution.py:19
  746.5 0.0 reduce-scatter.8.cloned.1.call-update
  746.6 69.2 %reduce-scatter.8.cloned.1.call-done = f32[16,12,128]{2,0,1:T(8,128)} async-done(((f32[128,12,128]{2,0,1:T(8,128)}), f32[16,12,128]{2,0,1:T(8,128)}) %reduce-scatter.8.cloned.1.call-update) | async-done | bytes 98320 | tf_op jit(solution)/shard_map/reduce_scatter | solution.py:47
  815.7 1.1 fusion.20
  816.9 0.7 pad_maximum_fusion
  (5 shorter events, 0.0 us)
Async XLA Ops:
  6.5 276.2 %copy-start = (f32[128,128]{1,0:T(8,128)S(1)}, f32[128,128]{1,0:T(8,128)}, u32[]{:S(2)}) copy-start(f32[128,128]{1,0:T(8,128)} %param.5) | copy-start | bytes 196612
  50.6 147.2 %all-to-all-start = ((f32[16,128,12,128]{3,1,2,0:T(8,128)}), f32[16,128,12,128]{3,1,2,0:T(8,128)}, u32[]{:S(2)}, u32[]{:S(2)}) async-start(f32[16,128,12,128]{3,1,2,0:T(8,128)} %stack.14), calls=%async_computation | async-start | bytes 25165824 | tf_op jit(solution)/shard_map/all_to_all | solution.py:13
  57.5 225.2 %copy-start.1 = (f32[16,12,128]{2,0,1:T(8,128)S(1)}, f32[16,12,128]{2,0,1:T(8,128)}, u32[]{:S(2)}) copy-start(f32[16,12,128]{2,0,1:T(8,128)} %param.3) | copy-start | bytes 294916
  57.5 225.2 %reduce-scatter.4.cloned.1.call-start = ((), (), s32[]{:S(2)}) async-start(), calls=%async_computation.6 | async-start | bytes 884736 | tf_op jit(solution)/shard_map/reduce_scatter | solution.py:47
  212.1 337.1 %reduce-scatter.6.cloned.1.call-start = ((), (), s32[]{:S(2)}) async-start(), calls=%async_computation.7 | async-start | bytes 884736 | tf_op jit(solution)/shard_map/reduce_scatter | solution.py:47
  321.1 146.4 %slice-start = ((s8[18874368]{0:T(1024)(128)(4,1)}), s8[4194304]{0:T(1024)(128)(4,1)S(1)}, s32[]{:S(2)}) async-start(s8[18874368]{0:T(1024)(128)(4,1)} %bitcast.66), calls=%async_computation.9 | async-start | bytes 8388608
  321.1 146.4 %slice-start.1 = ((s8[18874368]{0:T(1024)(128)(4,1)}), s8[2097152]{0:T(1024)(128)(4,1)S(1)}, s32[]{:S(2)}) async-start(s8[18874368]{0:T(1024)(128)(4,1)} %bitcast.66), calls=%async_computation.10 | async-start | bytes 4194304
  322.7 144.8 %slice-start.2 = ((s8[18874368]{0:T(1024)(128)(4,1)}), s8[4194304]{0:T(1024)(128)(4,1)S(1)}, s32[]{:S(2)}) async-start(s8[18874368]{0:T(1024)(128)(4,1)} %bitcast.66), calls=%async_computation.11 | async-start | bytes 8388608
  322.7 144.8 %slice-start.3 = ((s8[18874368]{0:T(1024)(128)(4,1)}), s8[4194304]{0:T(1024)(128)(4,1)S(1)}, s32[]{:S(2)}) async-start(s8[18874368]{0:T(1024)(128)(4,1)} %bitcast.66), calls=%async_computation.12 | async-start | bytes 8388608
  322.7 144.8 %slice-start.4 = ((s8[18874368]{0:T(1024)(128)(4,1)}), s8[4194304]{0:T(1024)(128)(4,1)S(1)}, s32[]{:S(2)}) async-start(s8[18874368]{0:T(1024)(128)(4,1)} %bitcast.66), calls=%async_computation.13 | async-start | bytes 8388608
  480.1 335.7 %reduce-scatter.8.cloned.1.call-start = ((), (), s32[]{:S(2)}) async-start(), calls=%async_computation.8 | async-start | bytes 884736 | tf_op jit(solution)/shard_map/reduce_scatter | solution.py:47
  587.6 146.4 %slice-start.5 = ((s8[18874368]{0:T(1024)(128)(4,1)}), s8[4194304]{0:T(1024)(128)(4,1)S(1)}, s32[]{:S(2)}) async-start(s8[18874368]{0:T(1024)(128)(4,1)} %bitcast.68), calls=%async_computation.14 | async-start | bytes 8388608
  587.6 146.4 %slice-start.6 = ((s8[18874368]{0:T(1024)(128)(4,1)}), s8[2097152]{0:T(1024)(128)(4,1)S(1)}, s32[]{:S(2)}) async-start(s8[18874368]{0:T(1024)(128)(4,1)} %bitcast.68), calls=%async_computation.15 | async-start | bytes 4194304
  589.2 144.8 %slice-start.7 = ((s8[18874368]{0:T(1024)(128)(4,1)}), s8[4194304]{0:T(1024)(128)(4,1)S(1)}, s32[]{:S(2)}) async-start(s8[18874368]{0:T(1024)(128)(4,1)} %bitcast.68), calls=%async_computation.16 | async-start | bytes 8388608
  589.2 144.8 %slice-start.8 = ((s8[18874368]{0:T(1024)(128)(4,1)}), s8[4194304]{0:T(1024)(128)(4,1)S(1)}, s32[]{:S(2)}) async-start(s8[18874368]{0:T(1024)(128)(4,1)} %bitcast.68), calls=%async_computation.17 | async-start | bytes 8388608
  589.2 144.8 %slice-start.9 = ((s8[18874368]{0:T(1024)(128)(4,1)}), s8[4194304]{0:T(1024)(128)(4,1)S(1)}, s32[]{:S(2)}) async-start(s8[18874368]{0:T(1024)(128)(4,1)} %bitcast.68), calls=%async_computation.18 | async-start | bytes 8388608
Sparse Core Ops, SparseCore 0:
  212.3 70.3 reduce-scatter.3
  480.2 68.9 reduce-scatter.5
  746.7 68.9 reduce-scatter.7
